TPU v7x, 128 devices: a whole 4x4x4 slice. The times are simulated.
128 devices in a mesh: aa: 16 (over x, z), ba: 8 (over y, core).
Axes of the slice: x: 4, y: 4, z: 4, core: 2. Of those that a mesh axis runs over, the one named last changes fastest.
Arguments:
- tokens: bfloat16 [2048, 3072], P('aa'), may hold values from -6 to 6
- cotangent: bfloat16 [2048, 3072], P('aa'), may hold values from -6 to 6
- route_scale: float32 [2048, 4], P('aa'), may hold values from 0.05 to 1
- expert_index: int32 [2048, 4], P('aa'), may hold values from 0 to 15, all different within a row; in each aligned block of 128 rows (0 to 127, 128 to 255, ...) at most 48 rows name the same one
- gate_matrix: bfloat16 [16, 3072, 5376], P('aa', None, 'ba'), may hold values from -0.15625 to 0.15625
- up_matrix: bfloat16 [16, 3072, 5376], P('aa', None, 'ba'), may hold values from -0.15625 to 0.15625
- down_matrix: bfloat16 [16, 5376, 3072], P('aa', 'ba'), may hold values from -0.078125 to 0.078125
Outputs:
- token_grad: bfloat16 [2048, 3072], P('aa', 'ba')
- gate_grad: bfloat16 [16, 3072, 5376], P('aa', None, 'ba')
- up_grad: bfloat16 [16, 3072, 5376], P('aa', None, 'ba')
- down_grad: bfloat16 [16, 5376, 3072], P('aa', 'ba')
Inputs may be any that keep to these rules, and one draw needn't show every extreme that they name: `expert_index`: each token names 4 different experts. Within each aligned block of 128 rows (the tokens of one index of aa) no expert is named more than 48 times, a bound that some block reaches.
All inputs are finite; a program needn't handle non-finite values.
Results may differ from a plain program's by a relative error of at most 0.02.
Values may be sent and summed in bfloat16 or wider, within the bound.
A program may use at most 192 MiB of HBM per device.

v0:
```python
import jax
import jax.numpy as jnp
from jax import lax
from jax.sharding import PartitionSpec as P


def slot_tables(expert_index, experts, capacity):
    assigned = expert_index.reshape(-1)
    labels = jnp.arange(experts, dtype=jnp.int32)
    onehot = (assigned[:, None] == labels[None, :]).astype(jnp.int32)
    earlier = jnp.cumsum(onehot, axis=0) - onehot
    ranking = jnp.sum(earlier * onehot, axis=1)
    target = assigned * capacity + ranking
    expert_loads = jnp.sum(onehot, axis=0)
    return (target, expert_loads)


def expert_pass(slot_rows, slot_scaled, gate_local, up_local, down_local):
    pre_gate = jnp.dot(slot_rows, gate_local, preferred_element_type=jnp.float32)
    pre_up = jnp.dot(slot_rows, up_local, preferred_element_type=jnp.float32)
    sigmoid_gate = jax.nn.sigmoid(pre_gate)
    activated = pre_gate * sigmoid_gate
    hidden = (activated * pre_up).astype(jnp.bfloat16)
    back_hidden = jnp.einsum(
        "rd,hd->rh", slot_scaled, down_local, preferred_element_type=jnp.float32
    )
    back_gate = (
        back_hidden * pre_up * sigmoid_gate * (1.0 + pre_gate * (1.0 - sigmoid_gate))
    ).astype(jnp.bfloat16)
    back_up = (back_hidden * activated).astype(jnp.bfloat16)
    grad_down = jnp.einsum("rh,rd->hd", hidden, slot_scaled, preferred_element_type=jnp.float32)
    grad_gate = jnp.einsum("rd,rh->dh", slot_rows, back_gate, preferred_element_type=jnp.float32)
    grad_up = jnp.einsum("rd,rh->dh", slot_rows, back_up, preferred_element_type=jnp.float32)
    partial_value = jnp.einsum(
        "rh,dh->rd", back_gate, gate_local, preferred_element_type=jnp.float32
    )
    partial_value = partial_value + jnp.einsum(
        "rh,dh->rd", back_up, up_local, preferred_element_type=jnp.float32
    )
    return (grad_gate, grad_up, grad_down, partial_value)


def shards(tokens, cotangent, route_scale, expert_index, gate_matrix, up_matrix, down_matrix):
    tok_rows, width = tokens.shape
    top_count = expert_index.shape[1]
    experts = lax.axis_size("aa")
    capacity = 3 * tok_rows * top_count // (2 * experts)
    slot_count = experts * capacity
    zero_value = jnp.zeros((), jnp.bfloat16)
    target, expert_loads = slot_tables(expert_index, experts, capacity)
    numbers = jnp.arange(tok_rows * top_count, dtype=jnp.int32)
    table = jnp.zeros((slot_count,), jnp.int32).at[target].set(numbers + 1)
    occupied = table > 0
    which_one = jnp.maximum(table - 1, 0)
    owner_row = which_one // top_count
    weight_rows = route_scale.reshape(-1)[which_one]
    send_rows = jnp.where(occupied[:, None], tokens[owner_row], zero_value).reshape(
        experts, capacity, width
    )
    scaled_rows = (weight_rows[:, None] * cotangent[owner_row].astype(jnp.float32)).astype(
        jnp.bfloat16
    )
    scaled_rows = jnp.where(occupied[:, None], scaled_rows, zero_value).reshape(
        experts, capacity, width
    )
    slot_rows, slot_scaled = (
        lax.all_to_all(send_rows, "aa", split_axis=0, concat_axis=0, tiled=True),
        lax.all_to_all(scaled_rows, "aa", split_axis=0, concat_axis=0, tiled=True),
    )
    slot_rows = slot_rows.reshape(slot_count, width)
    slot_scaled = slot_scaled.reshape(slot_count, width)
    gate_local = gate_matrix[0]
    up_local = up_matrix[0]
    down_local = down_matrix[0]
    grad_gate, grad_up, grad_down, partial_value = expert_pass(
        slot_rows, slot_scaled, gate_local, up_local, down_local
    )
    partial_rounded = partial_value.astype(jnp.bfloat16)
    returned = lax.all_to_all(
        partial_rounded.reshape(experts, capacity, width),
        "aa",
        split_axis=0,
        concat_axis=0,
        tiled=True,
    )
    summed = lax.psum_scatter(returned, "ba", scatter_dimension=2, tiled=True).astype(jnp.float32)
    slot_grad = summed.astype(jnp.bfloat16)
    slot_grad = slot_grad.reshape(slot_count, -1)
    gathered = slot_grad[target].reshape(tok_rows, top_count, -1).astype(jnp.float32)
    token_grad = jnp.sum(gathered, axis=1).astype(jnp.bfloat16)
    return (
        token_grad,
        grad_gate.astype(jnp.bfloat16)[None],
        grad_up.astype(jnp.bfloat16)[None],
        grad_down.astype(jnp.bfloat16)[None],
    )


def solution(mesh):
    in_specs = (
        P("aa", None),
        P("aa", None),
        P("aa", None),
        P("aa", None),
        P("aa", None, "ba"),
        P("aa", None, "ba"),
        P("aa", "ba", None),
    )
    out_specs = (P("aa", "ba"), P("aa", None, "ba"), P("aa", None, "ba"), P("aa", "ba", None))
    return jax.shard_map(shards, mesh=mesh, in_specs=in_specs, out_specs=out_specs, check_vma=False)
```

profile of v0, /device:TPU:0, one launch (start us, length us, event | category | flops | bytes accessed | tf_op | source)
XLA Modules:
  0.0 324.8 jit_solution(8172503425528347535)
XLA Ops:
  7.2 0.9 copy.17
  8.3 0.7 broadcast_multiply_fusion
  9.0 1.2 reduce-window.6
  10.1 0.2 slice_reduce_fusion
  10.4 0.1 copy.16
  10.5 0.1 mul.53
  10.7 2.4 scatter_custom_fusion
  13.2 5.1 %gather_fusion.1 = bf16[768,3072]{1,0:T(8,128)(2,1)} fusion(bf16[128,3072]{1,0:T(8,128)(2,1)S(1)} %copy-done, s32[1024]{0:T(1024)S(1)} %get-tuple-element.10), kind=kCustom, calls=%fused_computation.1 | custom fusion | bytes 9440256 | tf_op jit(solution)/shard_map/gather | solution.py:60
  18.3 5.0 %gather_fusion.2 = bf16[768,3072]{1,0:T(8,128)(2,1)} fusion(bf16[128,3072]{1,0:T(8,128)(2,1)S(1)} %copy-done.2, s32[1024]{0:T(1024)S(1)} %get-tuple-element.10), kind=kCustom, calls=%fused_computation.2 | custom fusion | bytes 9440256 | tf_op jit(solution)/shard_map/gather | solution.py:57
  23.3 0.1 copy.20
  23.5 5.0 %gather_fusion = f32[768]{0:T(1024)S(1)} fusion(f32[512]{0:T(512)S(1)} %reshape.95, s32[1024]{0:T(1024)S(1)} %get-tuple-element.11), kind=kCustom, calls=%fused_computation | custom fusion | bytes 9216 | tf_op jit(solution)/shard_map/gather | solution.py:56
  28.7 7.4 %fusion.1 = (bf16[16,48,3072]{2,1,0:T(8,128)(2,1)}, bf16[16,48,3072]{2,1,0:T(8,128)(2,1)S(1)}) fusion(bf16[16,48,3072]{2,1,0:T(8,128)(2,1)} %bitcast.63, f32[16,48]{1,0:T(8,128)S(1)} %mul.55, pred[16,48]{1,0:T(8,128)(4,1)S(1)} %broadcast_in_dim.40, bf16[16,48,3072]{2,1,0:T(8,128)(2,1)} %bitcast.64), kind=kLoop, calls=%fused_computation.11 | loop fusion | flops 11796480 | bytes 18878208 | tf_op jit(solution)/shard_map/jit(_where)/select_n | solution.py:63
  36.1 64.3 %all_to_all.15 = bf16[16,48,3072]{2,1,0:T(8,128)(2,1)} all-to-all(bf16[16,48,3072]{2,1,0:T(8,128)(2,1)S(1)} %get-tuple-element.9), channel_id=1, replica_groups=mesh['aa'=16,'ba'=8] {'aa'}, dimensions={0} | all-to-all | bytes 9437184 | tf_op jit(solution)/shard_map/all_to_all | solution.py:67
  100.4 4.7 %all-to-all-start = ((bf16[16,48,3072]{2,1,0:T(8,128)(2,1)}), bf16[16,48,3072]{2,1,0:T(8,128)(2,1)}, u32[]{:S(2)}, u32[]{:S(2)}) async-start(bf16[16,48,3072]{2,1,0:T(8,128)(2,1)} %get-tuple-element.8), calls=%async_computation | async-start | bytes 9437184 | tf_op jit(solution)/shard_map/all_to_all | solution.py:68
  105.1 0.2 reduce-scatter.4.cloned.1.call-start
  105.3 8.4 %fusion.10 = f32[768,672]{0,1:T(8,128)} fusion(bf16[768,3072]{1,0:T(8,128)(2,1)} %bitcast.66, bf16[1,3072,672]{1,2,0:T(8,128)(2,1)} %param.12), kind=kOutput, calls=%fused_computation.21 | convolution fusion | flops 3170893824 | bytes 10911744 | tf_op jit(solution)/shard_map/dot_general | solution.py:20
  113.8 4.8 %fusion.7 = f32[768,672]{0,1:T(8,128)} fusion(bf16[768,3072]{1,0:T(8,128)(2,1)S(1)} %bitcast.70, bf16[1,3072,672]{1,2,0:T(8,128)(2,1)S(1)} %copy-done.3), kind=kOutput, calls=%fused_computation.18 | convolution fusion | flops 3170893824 | bytes 10911744 | tf_op jit(solution)/shard_map/dot_general | solution.py:19
  118.5 47.2 %all-to-all-done = bf16[16,48,3072]{2,1,0:T(8,128)(2,1)} async-done(((bf16[16,48,3072]{2,1,0:T(8,128)(2,1)}), bf16[16,48,3072]{2,1,0:T(8,128)(2,1)}, u32[]{:S(2)}, u32[]{:S(2)}) %all-to-all-start) | async-done | bytes 4718624 | tf_op jit(solution)/shard_map/all_to_all | solution.py:68
  165.7 8.8 %multiply_convert_fusion.1 = (bf16[768,672]{0,1:T(8,128)(2,1)S(1)}, bf16[768,672]{0,1:T(8,128)(2,1)S(1)}) fusion(f32[768,672]{0,1:T(8,128)} %fusion.7, f32[768,672]{0,1:T(8,128)} %fusion.10, bf16[768,3072]{1,0:T(8,128)(2,1)} %bitcast.4, bf16[1,672,3072]{2,1,0:T(8,128)(2,1)} %param.13), kind=kOutput, calls=%fused_computation.26 | convolution fusion | flops 3177603072 | bytes 15040512 | tf_op jit(solution)/shard_map/rd,hd->rh/dot_general | solution.py:24
  174.5 3.9 %fusion.5 = f32[768,3072]{1,0:T(8,128)S(1)} fusion(bf16[768,672]{0,1:T(8,128)(2,1)S(1)} %get-tuple-element.5, bf16[1,3072,672]{1,2,0:T(8,128)(2,1)S(1)} %copy-done.4), kind=kOutput, calls=%fused_computation.16 | convolution fusion | flops 3170893824 | bytes 14598144 | tf_op jit(solution)/shard_map/rh,dh->rd/dot_general | solution.py:34
  178.5 4.4 %add_convert_fusion = bf16[768,3072]{1,0:T(8,128)(2,1)S(1)} fusion(f32[768,3072]{1,0:T(8,128)S(1)} %fusion.5, bf16[768,672]{0,1:T(8,128)(2,1)S(1)} %get-tuple-element.4, bf16[1,3072,672]{1,2,0:T(8,128)(2,1)S(1)} %copy-done.6), kind=kOutput, calls=%fused_computation.7 | convolution fusion | flops 3175612416 | bytes 19316736 | tf_op jit(solution)/shard_map/rh,dh->rd/dot_general | solution.py:37
  182.9 57.8 %all_to_all.16 = bf16[16,48,3072]{2,1,0:T(8,128)(2,1)} all-to-all(bf16[16,48,3072]{2,1,0:T(8,128)(2,1)S(1)} %bitcast.74), channel_id=1, replica_groups=mesh['aa'=16,'ba'=8] {'aa'}, dimensions={0} | all-to-all | bytes 9437184 | tf_op jit(solution)/shard_map/all_to_all | solution.py:79
  240.6 15.0 %copy.21 = bf16[16,48,3072]{1,0,2:T(8,128)(2,1)} copy(bf16[16,48,3072]{2,1,0:T(8,128)(2,1)} %all_to_all.16) | data formatting | bytes 9437184
  255.6 18.1 %reshape.145 = bf16[3072,768]{1,0:T(8,128)(2,1)} reshape(bf16[3072,16,48]{2,1,0:T(8,128)(2,1)} %bitcast.61) | data formatting | bytes 9437184
  273.8 7.4 %fusion.3 = bf16[1,3072,672]{1,2,0:T(8,128)(2,1)} fusion(bf16[768,672]{0,1:T(8,128)(2,1)S(1)} %get-tuple-element.5, bf16[768,3072]{1,0:T(8,128)(2,1)} %bitcast.67), kind=kOutput, calls=%fused_computation.14 | convolution fusion | flops 3172958208 | bytes 9879552 | tf_op jit(solution)/shard_map/rd,rh->dh/dot_general | solution.py:32
  281.2 4.9 %fusion.4 = bf16[1,3072,672]{1,2,0:T(8,128)(2,1)} fusion(bf16[768,672]{0,1:T(8,128)(2,1)S(1)} %copy-done.8, bf16[768,3072]{1,0:T(8,128)(2,1)S(1)} %bitcast.73), kind=kOutput, calls=%fused_computation.15 | convolution fusion | flops 3172958208 | bytes 9879552 | tf_op jit(solution)/shard_map/rd,rh->dh/dot_general | solution.py:33
  286.1 7.5 %fusion.2 = bf16[1,672,3072]{2,1,0:T(8,128)(2,1)} fusion(bf16[768,3072]{1,0:T(8,128)(2,1)} %bitcast.4, f32[768,672]{0,1:T(8,128)S(1)} %copy-done.9, f32[768,672]{0,1:T(8,128)S(1)} %copy-done.10), kind=kOutput, calls=%fused_computation.13 | convolution fusion | flops 3176054784 | bytes 12976128 | tf_op jit(solution)/shard_map/rh,rd->hd/dot_general | solution.py:31
  293.6 17.2 %reduce-scatter.4.cloned.1.call-done = bf16[384,768]{1,0:T(8,128)(2,1)} async-done(((bf16[3072,768]{1,0:T(8,128)(2,1)}), bf16[384,768]{1,0:T(8,128)(2,1)}) %reduce-scatter.4.cloned.1.call-update) | async-done | bytes 589840
  310.8 2.8 reshape.146
  313.6 1.2 copy.22
  314.7 1.9 gather_fusion.3
  316.8 1.1 reduce_sum.25
  (49 shorter events, 0.8 us)
Async XLA Ops:
  7.2 6.0 %copy-start = (bf16[128,3072]{1,0:T(8,128)(2,1)S(1)}, bf16[128,3072]{1,0:T(8,128)(2,1)}, u32[]{:S(2)}) copy-start(bf16[128,3072]{1,0:T(8,128)(2,1)} %param.8) | copy-start | bytes 2359300
  13.2 5.1 %copy-start.2 = (bf16[128,3072]{1,0:T(8,128)(2,1)S(1)}, bf16[128,3072]{1,0:T(8,128)(2,1)}, u32[]{:S(2)}) copy-start(bf16[128,3072]{1,0:T(8,128)(2,1)} %param.7) | copy-start | bytes 2359300
  18.3 5.0 %copy-start.5 = (f32[128,4]{0,1:T(4,128)S(1)}, f32[128,4]{0,1:T(4,128)}, u32[]{:S(2)}) copy-start(f32[128,4]{0,1:T(4,128)} %param.9) | copy-start | bytes 6148
  100.4 13.4 %slice-start = ((s8[4718592]{0:T(1024)(128)(4,1)}), s8[524288]{0:T(1024)(128)(4,1)S(1)}, s32[]{:S(2)}) async-start(s8[4718592]{0:T(1024)(128)(4,1)} %bitcast.68), calls=%async_computation.5 | async-start | bytes 1048576
  100.4 65.3 %all-to-all-start = ((bf16[16,48,3072]{2,1,0:T(8,128)(2,1)}), bf16[16,48,3072]{2,1,0:T(8,128)(2,1)}, u32[]{:S(2)}, u32[]{:S(2)}) async-start(bf16[16,48,3072]{2,1,0:T(8,128)(2,1)} %get-tuple-element.8), calls=%async_computation | async-start | bytes 9437184 | tf_op jit(solution)/shard_map/all_to_all | solution.py:68
  105.1 205.7 %reduce-scatter.4.cloned.1.call-start = ((), (), s32[]{:S(2)}) async-start(), calls=%async_computation.4 | async-start | bytes 5308416
  105.3 8.5 %slice-start.1 = ((s8[4718592]{0:T(1024)(128)(4,1)}), s8[4194304]{0:T(1024)(128)(4,1)S(1)}, s32[]{:S(2)}) async-start(s8[4718592]{0:T(1024)(128)(4,1)} %bitcast.68), calls=%async_computation.6 | async-start | bytes 8388608
  105.3 8.5 %copy-start.3 = (bf16[1,3072,672]{1,2,0:T(8,128)(2,1)S(1)}, bf16[1,3072,672]{1,2,0:T(8,128)(2,1)}, u32[]{:S(2)}) copy-start(bf16[1,3072,672]{1,2,0:T(8,128)(2,1)} %param.11) | copy-start | bytes 12386308
  165.7 8.8 %copy-start.4 = (bf16[1,3072,672]{1,2,0:T(8,128)(2,1)S(1)}, bf16[1,3072,672]{1,2,0:T(8,128)(2,1)}, u32[]{:S(2)}) copy-start(bf16[1,3072,672]{1,2,0:T(8,128)(2,1)} %param.11) | copy-start | bytes 12386308
  174.5 4.0 %copy-start.7 = (bf16[768,672]{0,1:T(8,128)(2,1)}, bf16[768,672]{0,1:T(8,128)(2,1)S(1)}, u32[]{:S(2)}) copy-start(bf16[768,672]{0,1:T(8,128)(2,1)S(1)} %get-tuple-element.4) | copy-start | bytes 3096580
  174.5 4.0 %copy-start.6 = (bf16[1,3072,672]{1,2,0:T(8,128)(2,1)S(1)}, bf16[1,3072,672]{1,2,0:T(8,128)(2,1)}, u32[]{:S(2)}) copy-start(bf16[1,3072,672]{1,2,0:T(8,128)(2,1)} %param.12) | copy-start | bytes 12386308
  273.7 7.5 %slice-start.2 = ((s8[4718592]{0:T(1024)(128)(4,1)}), s8[524288]{0:T(1024)(128)(4,1)S(1)}, s32[]{:S(2)}) async-start(s8[4718592]{0:T(1024)(128)(4,1)} %bitcast.71), calls=%async_computation.7 | async-start | bytes 1048576
  273.7 7.5 %slice-start.3 = ((s8[4718592]{0:T(1024)(128)(4,1)}), s8[4194304]{0:T(1024)(128)(4,1)S(1)}, s32[]{:S(2)}) async-start(s8[4718592]{0:T(1024)(128)(4,1)} %bitcast.71), calls=%async_computation.8 | async-start | bytes 8388608
  273.8 7.4 %copy-start.8 = (bf16[768,672]{0,1:T(8,128)(2,1)S(1)}, bf16[768,672]{0,1:T(8,128)(2,1)}, u32[]{:S(2)}) copy-start(bf16[768,672]{0,1:T(8,128)(2,1)} %copy-done.7) | copy-start | bytes 3096580
  281.2 4.9 %copy-start.9 = (f32[768,672]{0,1:T(8,128)S(1)}, f32[768,672]{0,1:T(8,128)}, u32[]{:S(2)}) copy-start(f32[768,672]{0,1:T(8,128)} %fusion.10) | copy-start | bytes 6193156
  281.2 4.9 %copy-start.10 = (f32[768,672]{0,1:T(8,128)S(1)}, f32[768,672]{0,1:T(8,128)}, u32[]{:S(2)}) copy-start(f32[768,672]{0,1:T(8,128)} %fusion.7) | copy-start | bytes 6193156
  286.1 31.8 %copy-start.1 = (bf16[128,3072]{1,0:T(8,128)(2,1)S(1)}, bf16[128,3072]{1,0:T(8,128)(2,1)}, u32[]{:S(2)}) copy-start(bf16[128,3072]{1,0:T(8,128)(2,1)} %param.8) | copy-start | bytes 2359300
Sparse Core Ops, SparseCore 0:
  273.8 36.8 reduce-scatter.3
where the time goes:
time: 326 us; the launch traced here: 325 us
  blocking collectives  122 us (37%)
  waiting for transfers between devices  64.3 us (20%)
  local copies, waits for them, and re-layouts  58.5 us (18%)
  matrix products  50.1 us (15%)
  between operations  14.3 us (4%)
  other arithmetic  10.6 us (3%)
  starting transfers between devices  4.91 us (2%)
    all_to_all x1, blocking collectives, shards(): lax.all_to_all(send_rows, 'aa', split_axis=0, concat_axis=0, tiled=True)  64.3 us
    all_to_all x1, blocking collectives, shards(): lax.all_to_all(partial_rounded.reshape(experts, capacity, width), 'aa', s...  57.8 us
    all_to_all x1, waiting for transfers between devices, shards(): lax.all_to_all(scaled_rows, 'aa', split_axis=0, concat_axis=0, tiled=True)  47.2 us
    unnamed x36, local copies, waits for them, and re-layouts  38 us
    unnamed x2, waiting for transfers between devices  17.2 us
    dot_general x1, matrix products, expert_pass(): jnp.einsum('rd,hd->rh', slot_scaled, down_local, preferred_element_type=j...  8.79 us
    dot_general x1, matrix products, expert_pass(): pre_up = jnp.dot(slot_rows, up_local, preferred_element_type=jnp.float32)  8.43 us
    dot_general x1, matrix products, expert_pass(): jnp.einsum('rh,rd->hd', hidden, slot_scaled, preferred_element_type=jnp.f...  7.49 us
  transfers between devices with their start and end apart: 2, of which 2 were waited for; matrix products, arithmetic and copies ran while one was open for 10% of the time, Pallas kernels for 0%

commit v1 on v0

v1 whole, which is shorter than its diff:
```python
import functools

import jax
import jax.numpy as jnp
from jax import lax
from jax.experimental import pallas as pl
from jax.experimental.pallas import tpu as pltpu
from jax.sharding import PartitionSpec as P

PIECES = 4
GRID = 4
BF16 = jnp.bfloat16
F32 = jnp.float32


def nt(a, b):
    return lax.dot_general(a, b, (((1,), (1,)), ((), ())), preferred_element_type=F32)


def tn(a, b):
    return lax.dot_general(a, b, (((0,), (0,)), ((), ())), preferred_element_type=F32)


def nn(a, b):
    return jnp.dot(a, b, preferred_element_type=F32)


def shifted(me, step, count, sign):
    if count != GRID * GRID:
        return lax.rem(me + sign * step + count, count)
    first = lax.rem(step, GRID)
    second = lax.rem(first + lax.div(step, GRID), GRID)
    row = lax.rem(lax.div(me, GRID) + sign * first + GRID, GRID)
    column = lax.rem(lax.rem(me, GRID) + sign * second + GRID, GRID)
    return row * GRID + column


def exchange_kernel(
    capacity,
    index_ref, scale_ref, tok_hbm, cot_hbm, gate_hbm, up_hbm, down_hbm,
    grad_ref, rows_hbm, act_hbm,
    rows, gate_v, up_v, down_v, piece, stage, select, rank, weight, total, act,
    to_pair, from_pair, to_y, keep, from_y, final, back, last_out, last_in,
    piece_sem, load_sem, xz_s, xz_r, pair_s, pair_r, y_s, y_r, rp_s, rp_r, ry_s, ry_r, rx_s, rx_r,
    last_sem, out_sem,
):
    count = lax.axis_size("aa")
    tokens = tok_hbm.shape[0]
    top = index_ref.shape[1]
    slots = count * capacity
    wide = rows.shape[3]
    width = wide // 2
    group = count // 4 if count >= 4 else 1
    chunks = count // group
    depth = group * capacity
    me = lax.axis_index("aa")
    b = lax.axis_index("ba")
    y, c = lax.div(b, 2), lax.rem(b, 2)
    h = lax.rem(y, 2)
    own = 2 * h + c
    other = 2 * (1 - h) + c
    pair = 2 * y + 1 - c
    after = 2 * lax.rem(y + 1, 4) + c
    before = 2 * lax.rem(y + 3, 4) + c
    across = lax.rem(b + 4, 8)

    barrier = pltpu.get_barrier_semaphore()

    def greet(step, carry):
        pl.semaphore_signal(barrier, inc=1, device_id={"aa": shifted(me, step, count, 1)}, device_id_type=pl.DeviceIdType.MESH)
        return carry

    lax.fori_loop(1, count, greet, 0)
    for neighbour in (pair, after, before, across):
        pl.semaphore_signal(barrier, inc=1, device_id={"ba": neighbour}, device_id_type=pl.DeviceIdType.MESH)

    def piece_load(array, half):
        source = (tok_hbm, cot_hbm)[array]
        start = pl.multiple_of((own + 4 * half) * width, 128)
        return pltpu.make_async_copy(
            source.at[:, pl.ds(start, width)], piece.at[array, :, pl.ds(half * width, width)], piece_sem.at[array, half])

    for array in range(2):
        for half in range(2):
            piece_load(array, half).start()

    def weight_loads(p):
        made = []
        for half in range(2):
            far = (p + 4 * half) * width
            near = half * width
            made.append(pltpu.make_async_copy(gate_hbm.at[0, pl.ds(far, width), :], gate_v.at[p, pl.ds(near, width), :], load_sem.at[0, half, p]))
            made.append(pltpu.make_async_copy(up_hbm.at[0, pl.ds(far, width), :], up_v.at[p, pl.ds(near, width), :], load_sem.at[1, half, p]))
            made.append(pltpu.make_async_copy(down_hbm.at[0, :, pl.ds(far, width)], down_v.at[p, :, pl.ds(near, width)], load_sem.at[2, half, p]))
        return made

    lane = lax.broadcasted_iota(jnp.int32, (tokens, 128), 1)
    packed = jnp.zeros((tokens, 128), F32)
    for k in range(top):
        packed = jnp.where(lane == k, index_ref[:, k : k + 1].astype(F32), packed)
        packed = jnp.where(lane == top + k, scale_ref[:, k : k + 1], packed)
    turned = packed.T
    labels = lax.broadcasted_iota(jnp.int32, (count, tokens), 0).astype(F32)
    chosen = jnp.zeros((count, tokens), F32)
    scales = jnp.zeros((count, tokens), F32)
    for k in range(top):
        hit = labels == turned[k : k + 1, :]
        chosen = jnp.where(hit, 1.0, chosen)
        scales = jnp.where(hit, turned[top + k : top + k + 1, :], scales)
    earlier = lax.broadcasted_iota(jnp.int32, (tokens, tokens), 0) < lax.broadcasted_iota(jnp.int32, (tokens, tokens), 1)
    ranks = nn(chosen.astype(BF16), jnp.where(earlier, 1.0, 0.0).astype(BF16))
    rank[...] = jnp.where(chosen > 0.5, ranks, -1.0)
    weight[...] = scales

    def remote(src, dst, send, recv, **where):
        return pltpu.make_async_remote_copy(
            src_ref=src, dst_ref=dst, send_sem=send, recv_sem=recv, device_id=where, device_id_type=pl.DeviceIdType.MESH)

    def block(o):
        return pl.ds(pl.multiple_of(o * capacity, 16), capacity)

    def chunk(q):
        return pl.ds(pl.multiple_of(q * depth, 16), depth)

    def xz(o):
        return remote(stage.at[o], rows.at[:, own, block(o), :], xz_s.at[o], xz_r.at[o], aa=shifted(me, o, count, 1))

    def to_core(k, o):
        there = rows.at[:, (own, other)[k], block(o), :]
        return remote(there, there, pair_s.at[k, o], pair_r.at[k, o], ba=pair)

    def to_plane(k, o):
        there = rows.at[:, own, block(o), pl.ds(k * width, width)]
        return remote(there, there, y_s.at[k, o], y_r.at[k, o], ba=(after, before)[k])

    def sum_core(k, q):
        return remote(to_pair.at[k, chunk(q), :], from_pair.at[k, chunk(q), :], rp_s.at[k, q], rp_r.at[k, q], ba=pair)

    def sum_plane(k, q):
        half = pl.ds(k * width, width)
        return remote(to_y.at[chunk(q), half], from_y.at[chunk(q), half], ry_s.at[k, q], ry_r.at[k, q], ba=(before, after)[k])

    def home(o):
        return remote(final.at[block(o), :], back.at[block(o), :], rx_s.at[o], rx_r.at[o], aa=shifted(me, o, count, -1))

    def rows_out(q):
        return [pltpu.make_async_copy(rows.at[a, :, chunk(q), :], rows_hbm.at[a, :, chunk(q), :], out_sem.at[a, q]) for a in range(2)]

    def act_out(q):
        return pltpu.make_async_copy(act.at[:, chunk(q), :], act_hbm.at[:, chunk(q), :], out_sem.at[2, q])

    for array in range(2):
        for half in range(2):
            piece_load(array, half).wait()
    for p in range(PIECES):
        for load in weight_loads(p):
            load.start()
    pl.semaphore_wait(barrier, count - 1 + 4)

    def dispatch(step, carry):
        o = lax.rem(step + 1, count)
        expert = shifted(me, o, count, 1)
        hits = rank[pl.ds(expert, 1), :] == lax.broadcasted_iota(jnp.int32, (capacity, tokens), 0).astype(F32)
        picks = jnp.where(hits, 1.0, 0.0)
        scale = jnp.sum(picks * weight[pl.ds(expert, 1), :], axis=1, keepdims=True)
        picks = picks.astype(BF16)
        select[block(o), :] = picks
        stage[o, 0] = nn(picks, piece[0]).astype(BF16)
        stage[o, 1] = (scale * nn(picks, piece[1])).astype(BF16)

        @pl.when(o > 0)
        def _():
            xz(o).start()

        @pl.when(o == 0)
        def _():
            for a in range(2):
                rows[a, own, 0:capacity, :] = stage[0, a]

        return carry

    lax.fori_loop(0, count, dispatch, 0)
    for p in range(PIECES):
        for load in weight_loads(p):
            load.wait()

    lag_c = group + 2
    lag_d = lag_c + 4
    lag_e = lag_d + 6
    steps = lag_e + 4 * (chunks - 1) + 1

    def main(t, carry):
        @pl.when(t < count)
        def _():
            @pl.when(t > 0)
            def _():
                xz(t).wait_recv()

            to_plane(0, t).start()
            to_plane(1, t).start()
            to_core(0, t).start()

        u = t - 1

        @pl.when((u >= 0) & (u < count))
        def _():
            to_plane(0, u).wait_recv()
            to_plane(1, u).wait_recv()
            to_core(1, u).start()

        v = t - lag_c

        @pl.when((v >= 0) & (v < 4 * chunks))
        def _():
            q, j = lax.div(v, 4), lax.rem(v, 4)

            @pl.when(j == 0)
            def _():
                for i in range(group):
                    to_core(0, q * group + i).wait_recv()
                    to_core(1, q * group + i).wait_recv()
                for copy in rows_out(q):
                    copy.start()
                total[...] = jnp.zeros_like(total)

            x = rows[0, j, chunk(q), :]
            total[0] += nn(x, gate_v[j])
            total[1] += nn(x, up_v[j])
            total[2] += nt(rows[1, j, chunk(q), :], down_v[j])

            @pl.when(j == 3)
            def _():
                gate, up, behind = total[0], total[1], total[2]
                sigmoid = jax.nn.sigmoid(gate)
                active = gate * sigmoid
                act[0, chunk(q), :] = (active * up).astype(BF16)
                act[1, chunk(q), :] = (behind * up * sigmoid * (1.0 + gate * (1.0 - sigmoid))).astype(BF16)
                act[2, chunk(q), :] = (behind * active).astype(BF16)
                act_out(q).start()

        w = t - lag_d

        @pl.when((w >= 0) & (w < 4 * chunks))
        def _():
            q, j = lax.div(w, 4), lax.rem(w, 4)
            plane = jnp.where(lax.rem(j, 2) == 0, 1 - h, h)
            core = jnp.where(j < 2, 1 - c, c)
            p = 2 * plane + core
            part = nt(act[1, chunk(q), :], gate_v[p]) + nt(act[2, chunk(q), :], up_v[p])

            @pl.when(j < 2)
            def _():
                to_pair[j, chunk(q), :] = part.astype(BF16)
                sum_core(j, q).start()

            @pl.when(j == 2)
            def _():
                sum_core(0, q).wait_recv()
                to_y[chunk(q), :] = (part + from_pair[0, chunk(q), :].astype(F32)).astype(BF16)
                sum_plane(0, q).start()
                sum_plane(1, q).start()

            @pl.when(j == 3)
            def _():
                sum_core(1, q).wait_recv()
                keep[chunk(q), :] = part + from_pair[1, chunk(q), :].astype(F32)

        z = t - lag_e

        @pl.when((z >= 0) & (lax.rem(z + 4, 4) == 0))
        def _():
            q = lax.div(z, 4)
            sum_plane(0, q).wait_recv()
            sum_plane(1, q).wait_recv()
            final[chunk(q), :] = (keep[chunk(q), :] + from_y[chunk(q), :].astype(F32)).astype(BF16)
            for i in range(group):
                o = q * group + i

                @pl.when(o > 0)
                def _():
                    home(o).start()

                @pl.when(o == 0)
                def _():
                    back[0:capacity, :] = final[0:capacity, :]

        return carry

    lax.fori_loop(0, steps, main, 0)

    def arrive(o, carry):
        home(o).wait_recv()
        return carry

    lax.fori_loop(1, count, arrive, 0)
    merged = tn(select[...], back[...])
    low, high = merged[:, :width], merged[:, width:]
    last_out[...] = jnp.where(y < 2, high, low).astype(BF16)
    swap = remote(last_out, last_in, last_sem.at[0], last_sem.at[1], ba=across)
    swap.start()
    mine = jnp.where(y < 2, low, high)
    swap.wait_recv()
    grad_ref[...] = (mine + last_in[...].astype(F32)).astype(BF16)
    swap.wait_send()

    def settle(o, carry):
        @pl.when(o > 0)
        def _():
            xz(o).wait_send()
            home(o).wait_send()

        for k in range(2):
            to_core(k, o).wait_send()
            to_plane(k, o).wait_send()
        return carry

    lax.fori_loop(0, count, settle, 0)

    def settle_sums(q, carry):
        for k in range(2):
            sum_core(k, q).wait_send()
            sum_plane(k, q).wait_send()
        for copy in rows_out(q):
            copy.wait()
        act_out(q).wait()
        return carry

    lax.fori_loop(0, chunks, settle_sums, 0)


def weight_grads_kernel(rows_ref, scaled_ref, act_ref, gate_ref, up_ref, down_ref):
    x, s = rows_ref[0, 0], scaled_ref[0, 0]
    gate_ref[0] = tn(x, act_ref[1]).astype(BF16)
    up_ref[0] = tn(x, act_ref[2]).astype(BF16)
    down_ref[0] = tn(act_ref[0], s).astype(BF16)


def shards(tokens, cotangent, route_scale, expert_index, gate_matrix, up_matrix, down_matrix):
    rows_here, features = tokens.shape
    top = expert_index.shape[1]
    experts = lax.axis_size("aa")
    capacity = 3 * rows_here * top // (2 * experts)
    slots = experts * capacity
    width = features // 8
    wide = 2 * width
    hidden = gate_matrix.shape[2]
    group = experts // 4 if experts >= 4 else 1
    chunks = experts // group
    depth = group * capacity
    any_, vmem, dma = pl.ANY, pltpu.VMEM, pltpu.SemaphoreType.DMA
    token_grad, slot_rows, acts = pl.pallas_call(
        functools.partial(exchange_kernel, capacity),
        out_shape=(
            jax.ShapeDtypeStruct((rows_here, width), BF16),
            jax.ShapeDtypeStruct((2, PIECES, slots, wide), BF16),
            jax.ShapeDtypeStruct((3, slots, hidden), BF16),
        ),
        in_specs=[pl.BlockSpec(memory_space=vmem)] * 2 + [pl.BlockSpec(memory_space=any_)] * 5,
        out_specs=(pl.BlockSpec(memory_space=vmem), pl.BlockSpec(memory_space=any_), pl.BlockSpec(memory_space=any_)),
        scratch_shapes=[
            vmem((2, PIECES, slots, wide), BF16),
            vmem((PIECES, wide, hidden), BF16),
            vmem((PIECES, wide, hidden), BF16),
            vmem((PIECES, hidden, wide), BF16),
            vmem((2, rows_here, wide), BF16),
            vmem((experts, 2, capacity, wide), BF16),
            vmem((slots, rows_here), BF16),
            vmem((experts, rows_here), F32),
            vmem((experts, rows_here), F32),
            vmem((3, depth, hidden), F32),
            vmem((3, slots, hidden), BF16),
            vmem((2, slots, wide), BF16),
            vmem((2, slots, wide), BF16),
            vmem((slots, wide), BF16),
            vmem((slots, wide), F32),
            vmem((slots, wide), BF16),
            vmem((slots, wide), BF16),
            vmem((slots, wide), BF16),
            vmem((rows_here, width), BF16),
            vmem((rows_here, width), BF16),
            dma((2, 2)),
            dma((3, 2, PIECES)),
            dma((experts,)),
            dma((experts,)),
            dma((2, experts)),
            dma((2, experts)),
            dma((2, experts)),
            dma((2, experts)),
            dma((2, chunks)),
            dma((2, chunks)),
            dma((2, chunks)),
            dma((2, chunks)),
            dma((experts,)),
            dma((experts,)),
            dma((2,)),
            dma((3, chunks)),
        ],
        compiler_params=pltpu.CompilerParams(
            collective_id=0, has_side_effects=True, vmem_limit_bytes=56 * 2**20
        ),
        cost_estimate=pl.CostEstimate(
            flops=10 * slots * features * hidden,
            bytes_accessed=6 * features * hidden + 4 * slots * features,
            transcendentals=slots * hidden,
        ),
    )(expert_index, route_scale, tokens, cotangent, gate_matrix, up_matrix, down_matrix)
    gate_grad, up_grad, down_grad = pl.pallas_call(
        weight_grads_kernel,
        grid=(8,),
        out_shape=(
            jax.ShapeDtypeStruct((1, features, hidden), BF16),
            jax.ShapeDtypeStruct((1, features, hidden), BF16),
            jax.ShapeDtypeStruct((1, hidden, features), BF16),
        ),
        in_specs=[
            pl.BlockSpec((1, 1, slots, width), lambda i: (0, lax.rem(i, 4), 0, lax.div(i, 4))),
            pl.BlockSpec((1, 1, slots, width), lambda i: (1, lax.rem(i, 4), 0, lax.div(i, 4))),
            pl.BlockSpec((3, slots, hidden), lambda i: (0, 0, 0)),
        ],
        out_specs=(
            pl.BlockSpec((1, width, hidden), lambda i: (0, i, 0)),
            pl.BlockSpec((1, width, hidden), lambda i: (0, i, 0)),
            pl.BlockSpec((1, hidden, width), lambda i: (0, 0, i)),
        ),
        compiler_params=pltpu.CompilerParams(vmem_limit_bytes=48 * 2**20),
        cost_estimate=pl.CostEstimate(
            flops=6 * slots * features * hidden,
            bytes_accessed=6 * features * hidden + 4 * slots * features,
            transcendentals=0,
        ),
    )(slot_rows, slot_rows, acts)
    return token_grad, gate_grad, up_grad, down_grad


def solution(mesh):
    in_specs = (
        P("aa", None),
        P("aa", None),
        P("aa", None),
        P("aa", None),
        P("aa", None, "ba"),
        P("aa", None, "ba"),
        P("aa", "ba", None),
    )
    out_specs = (P("aa", "ba"), P("aa", None, "ba"), P("aa", None, "ba"), P("aa", "ba", None))
    return jax.shard_map(shards, mesh=mesh, in_specs=in_specs, out_specs=out_specs, check_vma=False)
```

time: 326 us -> 146 us (0.45)
  blocking collectives: 122 us -> 0 us
  Pallas kernels: 0 us -> 112 us
  waiting for transfers between devices: 64.3 us -> 0 us
  matrix products: 50.1 us -> 0 us
  local copies, waits for them, and re-layouts: 58.5 us -> 31.2 us
  between operations: 14.3 us -> 0.65 us
  other arithmetic: 10.6 us -> 0 us
  starting transfers between devices: 4.91 us -> 0 us
    all_to_all x2 -> x0, blocking collectives: 122 us -> none  [the longest x1 64.3 us: shards(): lax.all_to_all(send_rows, 'aa', split_axis=0, concat_axis=0, tiled=True)]
    pallas_call x0 -> x2, Pallas kernels: none -> 112 us  [the longest x1 96.9 us: shards(): pl.pallas_call(functools.partial(exchange_kernel, capacity), out_shape=(j...]
    dot_general x8 -> x0, matrix products: 50.1 us -> none  [the longest x1 8.79 us: expert_pass(): jnp.einsum('rd,hd->rh', slot_scaled, down_local, preferred_element_type=j...]
    all_to_all x1 -> x0, waiting for transfers between devices: 47.2 us -> none  [shards(): lax.all_to_all(scaled_rows, 'aa', split_axis=0, concat_axis=0, tiled=True)]
    unnamed x2 -> x0, waiting for transfers between devices: 17.2 us -> none
    gather x4 -> x0, local copies, waits for them, and re-layouts: 17 us -> none  [the longest x1 5.07 us: shards(): cotangent[owner_row].astype(jnp.float32)]
    select_n x2 -> x0, other arithmetic: 7.41 us -> none  [the longest x1 7.4 us: shards(): jnp.where(occupied[:, None], scaled_rows, zero_value)]
    unnamed x36 -> x11, local copies, waits for them, and re-layouts: 38 us -> 31.2 us
  transfers between devices with their start and end apart: 2 -> 0, of which waited for: 2 -> 0; matrix products, arithmetic and copies ran while one was open for 10% -> 0% of each run, Pallas kernels for 0% -> 0%
where the time goes in v1:
time: 146 us; the launch traced here: 144 us
  Pallas kernels  112 us (77%)
  local copies, waits for them, and re-layouts  31.2 us (21%)
    pallas_call x1, Pallas kernels, shards(): pl.pallas_call(functools.partial(exchange_kernel, capacity), out_shape=(j...  96.9 us
    unnamed x11, local copies, waits for them, and re-layouts  31.2 us
    pallas_call x1, Pallas kernels, shards(): pl.pallas_call(weight_grads_kernel, grid=(8,), out_shape=(jax.ShapeDtypeS...  15.4 us

profile of v1, /device:TPU:0, one launch (start us, length us, event | category | flops | bytes accessed | tf_op | source)
XLA Modules:
  0.0 144.2 jit_solution(14870049066095597254)
XLA Ops:
  0.6 1.4 copy.12.scale_ref
  2.0 1.4 copy.11.index_ref
  3.5 6.4 %copy.13.gate_hbm = bf16[1,3072,672]{2,1,0:T(8,128)(2,1)} copy(bf16[1,3072,672]{1,2,0:T(8,128)(2,1)} %param.11) | data formatting | bytes 8257536 | tf_op args[4]
  9.9 6.5 %copy.14.up_hbm = bf16[1,3072,672]{2,1,0:T(8,128)(2,1)} copy(bf16[1,3072,672]{1,2,0:T(8,128)(2,1)} %param.12) | data formatting | bytes 8257536 | tf_op args[5]
  16.4 96.9 %shard_map.102 = (bf16[128,384]{1,0:T(8,128)(2,1)}, bf16[2,4,768,768]{3,2,1,0:T(8,128)(2,1)}, bf16[3,768,672]{2,1,0:T(8,128)(2,1)}) custom-call(s32[128,4]{1,0:T(8,128)} %copy.11.index_ref, f32[128,4]{1,0:T(8,128)} %copy.12.scale_ref, bf16[128,3072]{1,0:T(8,128)(2,1)} %tok_hbm.1, bf16[128,3072]{1,0:T(8,128)(2,1)} %cot_hbm.1, ...), custom_call_target="tpu_custom_call" | custom-call | flops 15854469120 | bytes 21823488 | tf_op jit(solution)/shard_map/pallas_call | solution.py:351
  113.2 0.0 copy-start
  113.2 2.0 %copy-done = bf16[3,768,672]{2,1,0:T(8,128)(2,1)S(1)} copy-done((bf16[3,768,672]{2,1,0:T(8,128)(2,1)S(1)}, bf16[3,768,672]{2,1,0:T(8,128)(2,1)}, u32[]{:S(2)}) %copy-start) | copy-done | bytes 3096600
  115.2 15.4 %shard_map.103 = (bf16[1,3072,672]{2,1,0:T(8,128)(2,1)}, bf16[1,3072,672]{2,1,0:T(8,128)(2,1)}, bf16[1,672,3072]{2,1,0:T(8,128)(2,1)}) custom-call(bf16[2,4,768,768]{3,2,1,0:T(8,128)(2,1)} %get-tuple-element.11.rows_ref.scaled_ref, bf16[2,4,768,768]{3,2,1,0:T(8,128)(2,1)} %get-tuple-element.11.rows_ref.scaled_ref, bf16[3,768,672]{2,1,0:T(8,128)(2,1)S(1)} %copy-done), custom_call_target="tpu_custom_call" | custom-call | flops 9512681472 | bytes 21823488 | tf_op jit(solution)/shard_map/pallas_call | solution.py:407
  130.7 6.4 %copy.15 = bf16[1,3072,672]{1,2,0:T(8,128)(2,1)} copy(bf16[1,3072,672]{2,1,0:T(8,128)(2,1)} %get-tuple-element.17) | data formatting | bytes 8257536
  137.1 0.0 copy-start.1
  137.1 6.4 %copy.16 = bf16[1,3072,672]{1,2,0:T(8,128)(2,1)} copy(bf16[1,3072,672]{2,1,0:T(8,128)(2,1)} %get-tuple-element.18) | data formatting | bytes 8257536
  143.5 0.0 copy-done.1
  143.5 0.6 copy.18
Async XLA Ops:
  113.2 2.0 %copy-start = (bf16[3,768,672]{2,1,0:T(8,128)(2,1)S(1)}, bf16[3,768,672]{2,1,0:T(8,128)(2,1)}, u32[]{:S(2)}) copy-start(bf16[3,768,672]{2,1,0:T(8,128)(2,1)} %get-tuple-element.12.act_ref) | copy-start | bytes 9289732
  137.1 6.4 %copy-start.1 = (bf16[128,384]{1,0:T(8,128)(2,1)S(1)}, bf16[128,384]{1,0:T(8,128)(2,1)}, u32[]{:S(2)}) copy-start(bf16[128,384]{1,0:T(8,128)(2,1)} %get-tuple-element.24) | copy-start | bytes 294916

commit v2 on v1

--- a/solution.py
+++ b/solution.py
@@ -9,6 +9,10 @@
 
 PIECES = 4
 GRID = 4
+AHEAD = 5
+RELAY_LAG = 3
+SLOTS_OUT = 4
+CUTS = (3, 8)
 BF16 = jnp.bfloat16
 F32 = jnp.float32
 
@@ -38,15 +42,15 @@
 def exchange_kernel(
     capacity,
     index_ref, scale_ref, tok_hbm, cot_hbm, gate_hbm, up_hbm, down_hbm,
-    grad_ref, rows_hbm, act_hbm,
+    grad_ref, weights_hbm,
     rows, gate_v, up_v, down_v, piece, stage, select, rank, weight, total, act,
-    to_pair, from_pair, to_y, keep, from_y, final, back, last_out, last_in,
+    to_pair, from_pair, to_y, keep, from_y, final, back, last_mine, last_out, last_in, turned, made,
     piece_sem, load_sem, xz_s, xz_r, pair_s, pair_r, y_s, y_r, rp_s, rp_r, ry_s, ry_r, rx_s, rx_r,
     last_sem, out_sem,
 ):
     count = lax.axis_size("aa")
     tokens = tok_hbm.shape[0]
-    top = index_ref.shape[1]
+    top = index_ref.shape[0]
     slots = count * capacity
     wide = rows.shape[3]
     width = wide // 2
@@ -89,24 +93,17 @@
         for half in range(2):
             far = (p + 4 * half) * width
             near = half * width
-            made.append(pltpu.make_async_copy(gate_hbm.at[0, pl.ds(far, width), :], gate_v.at[p, pl.ds(near, width), :], load_sem.at[0, half, p]))
-            made.append(pltpu.make_async_copy(up_hbm.at[0, pl.ds(far, width), :], up_v.at[p, pl.ds(near, width), :], load_sem.at[1, half, p]))
-            made.append(pltpu.make_async_copy(down_hbm.at[0, :, pl.ds(far, width)], down_v.at[p, :, pl.ds(near, width)], load_sem.at[2, half, p]))
+            for k, (source, target) in enumerate(((gate_hbm, gate_v), (up_hbm, up_v), (down_hbm, down_v))):
+                made.append(pltpu.make_async_copy(source.at[0, :, pl.ds(far, width)], target.at[p, :, pl.ds(near, width)], load_sem.at[k, half, p]))
         return made
 
-    lane = lax.broadcasted_iota(jnp.int32, (tokens, 128), 1)
-    packed = jnp.zeros((tokens, 128), F32)
-    for k in range(top):
-        packed = jnp.where(lane == k, index_ref[:, k : k + 1].astype(F32), packed)
-        packed = jnp.where(lane == top + k, scale_ref[:, k : k + 1], packed)
-    turned = packed.T
-    labels = lax.broadcasted_iota(jnp.int32, (count, tokens), 0).astype(F32)
+    labels = lax.broadcasted_iota(jnp.int32, (count, tokens), 0)
     chosen = jnp.zeros((count, tokens), F32)
     scales = jnp.zeros((count, tokens), F32)
     for k in range(top):
-        hit = labels == turned[k : k + 1, :]
+        hit = labels == index_ref[k : k + 1, :]
         chosen = jnp.where(hit, 1.0, chosen)
-        scales = jnp.where(hit, turned[top + k : top + k + 1, :], scales)
+        scales = jnp.where(hit, scale_ref[k : k + 1, :], scales)
     earlier = lax.broadcasted_iota(jnp.int32, (tokens, tokens), 0) < lax.broadcasted_iota(jnp.int32, (tokens, tokens), 1)
     ranks = nn(chosen.astype(BF16), jnp.where(earlier, 1.0, 0.0).astype(BF16))
     rank[...] = jnp.where(chosen > 0.5, ranks, -1.0)
@@ -143,11 +140,29 @@
     def home(o):
         return remote(final.at[block(o), :], back.at[block(o), :], rx_s.at[o], rx_r.at[o], aa=shifted(me, o, count, -1))
 
-    def rows_out(q):
-        return [pltpu.make_async_copy(rows.at[a, :, chunk(q), :], rows_hbm.at[a, :, chunk(q), :], out_sem.at[a, q]) for a in range(2)]
-
-    def act_out(q):
-        return pltpu.make_async_copy(act.at[:, chunk(q), :], act_hbm.at[:, chunk(q), :], out_sem.at[2, q])
+    def grad_out(n, half):
+        k, p = lax.rem(n, 3), lax.div(n, 3)
+        slot = lax.rem(n, SLOTS_OUT)
+        there = pl.ds(pl.multiple_of((p + 4 * half) * width, 128), width)
+        return pltpu.make_async_copy(
+            made.at[slot, :, pl.ds(half * width, width)], weights_hbm.at[k, :, there], out_sem.at[slot, half])
+
+    def grad_step(n, carry):
+        k, p = lax.rem(n, 3), lax.div(n, 3)
+
+        @pl.when(n >= SLOTS_OUT)
+        def _():
+            for half in range(2):
+                grad_out(n - SLOTS_OUT, half).wait()
+
+        side = jnp.where(k == 0, 1, 0)
+        made[lax.rem(n, SLOTS_OUT)] = nn(turned[k], rows[side, p]).astype(BF16)
+        for half in range(2):
+            grad_out(n, half).start()
+        return carry
+
+    def grads(first, last):
+        lax.fori_loop(first, last, grad_step, 0)
 
     for array in range(2):
         for half in range(2):
@@ -168,7 +183,7 @@
         stage[o, 0] = nn(picks, piece[0]).astype(BF16)
         stage[o, 1] = (scale * nn(picks, piece[1])).astype(BF16)
 
-        @pl.when(o > 0)
+        @pl.when((o > 0) & (o < AHEAD))
         def _():
             xz(o).start()
 
@@ -184,10 +199,25 @@
         for load in weight_loads(p):
             load.wait()
 
-    lag_c = group + 2
+    lag_c = group + RELAY_LAG + 1
     lag_d = lag_c + 4
     lag_e = lag_d + 6
-    steps = lag_e + 4 * (chunks - 1) + 1
+    steps = lag_d + 4 * chunks
+
+    def send_home(q):
+        sum_plane(0, q).wait_recv()
+        sum_plane(1, q).wait_recv()
+        final[chunk(q), :] = (keep[chunk(q), :] + from_y[chunk(q), :].astype(F32)).astype(BF16)
+        for i in range(group):
+            o = q * group + i
+
+            @pl.when(o > 0)
+            def _():
+                home(o).start()
+
+            @pl.when(o == 0)
+            def _():
+                back[0:capacity, :] = final[0:capacity, :]
 
     def main(t, carry):
         @pl.when(t < count)
@@ -200,7 +230,15 @@
             to_plane(1, t).start()
             to_core(0, t).start()
 
-        u = t - 1
+            @pl.when(t + AHEAD < count)
+            def _():
+                @pl.when(t > 0)
+                def _():
+                    xz(t).wait_send()
+
+                xz(t + AHEAD).start()
+
+        u = t - RELAY_LAG
 
         @pl.when((u >= 0) & (u < count))
         def _():
@@ -219,13 +257,11 @@
                 for i in range(group):
                     to_core(0, q * group + i).wait_recv()
                     to_core(1, q * group + i).wait_recv()
-                for copy in rows_out(q):
-                    copy.start()
                 total[...] = jnp.zeros_like(total)
 
             x = rows[0, j, chunk(q), :]
-            total[0] += nn(x, gate_v[j])
-            total[1] += nn(x, up_v[j])
+            total[0] += nt(x, gate_v[j])
+            total[1] += nt(x, up_v[j])
             total[2] += nt(rows[1, j, chunk(q), :], down_v[j])
 
             @pl.when(j == 3)
@@ -236,7 +272,6 @@
                 act[0, chunk(q), :] = (active * up).astype(BF16)
                 act[1, chunk(q), :] = (behind * up * sigmoid * (1.0 + gate * (1.0 - sigmoid))).astype(BF16)
                 act[2, chunk(q), :] = (behind * active).astype(BF16)
-                act_out(q).start()
 
         w = t - lag_d
 
@@ -246,7 +281,7 @@
             plane = jnp.where(lax.rem(j, 2) == 0, 1 - h, h)
             core = jnp.where(j < 2, 1 - c, c)
             p = 2 * plane + core
-            part = nt(act[1, chunk(q), :], gate_v[p]) + nt(act[2, chunk(q), :], up_v[p])
+            part = nn(act[1, chunk(q), :], gate_v[p]) + nn(act[2, chunk(q), :], up_v[p])
 
             @pl.when(j < 2)
             def _():
@@ -267,26 +302,22 @@
 
         z = t - lag_e
 
-        @pl.when((z >= 0) & (lax.rem(z + 4, 4) == 0))
-        def _():
-            q = lax.div(z, 4)
-            sum_plane(0, q).wait_recv()
-            sum_plane(1, q).wait_recv()
-            final[chunk(q), :] = (keep[chunk(q), :] + from_y[chunk(q), :].astype(F32)).astype(BF16)
-            for i in range(group):
-                o = q * group + i
-
-                @pl.when(o > 0)
-                def _():
-                    home(o).start()
-
-                @pl.when(o == 0)
-                def _():
-                    back[0:capacity, :] = final[0:capacity, :]
+        @pl.when((z >= 0) & (z < 4 * (chunks - 1)) & (lax.rem(z + 4, 4) == 0))
+        def _():
+            send_home(lax.div(z, 4))
 
         return carry
 
     lax.fori_loop(0, steps, main, 0)
+
+    def turn(k, carry):
+        turned[k] = act[k].T
+        return carry
+
+    lax.fori_loop(0, 3, turn, 0)
+    grads(0, CUTS[0])
+    send_home(chunks - 1)
+    grads(CUTS[0], CUTS[1])
 
     def arrive(o, carry):
         home(o).wait_recv()
@@ -296,17 +327,18 @@
     merged = tn(select[...], back[...])
     low, high = merged[:, :width], merged[:, width:]
     last_out[...] = jnp.where(y < 2, high, low).astype(BF16)
+    last_mine[...] = jnp.where(y < 2, low, high)
     swap = remote(last_out, last_in, last_sem.at[0], last_sem.at[1], ba=across)
     swap.start()
-    mine = jnp.where(y < 2, low, high)
-    swap.wait_recv()
-    grad_ref[...] = (mine + last_in[...].astype(F32)).astype(BF16)
-    swap.wait_send()
+    grads(CUTS[1], 3 * PIECES)
 
     def settle(o, carry):
+        @pl.when((o > 0) & (o >= count - AHEAD))
+        def _():
+            xz(o).wait_send()
+
         @pl.when(o > 0)
         def _():
-            xz(o).wait_send()
             home(o).wait_send()
 
         for k in range(2):
@@ -320,19 +352,19 @@
         for k in range(2):
             sum_core(k, q).wait_send()
             sum_plane(k, q).wait_send()
-        for copy in rows_out(q):
-            copy.wait()
-        act_out(q).wait()
         return carry
 
     lax.fori_loop(0, chunks, settle_sums, 0)
-
-
-def weight_grads_kernel(rows_ref, scaled_ref, act_ref, gate_ref, up_ref, down_ref):
-    x, s = rows_ref[0, 0], scaled_ref[0, 0]
-    gate_ref[0] = tn(x, act_ref[1]).astype(BF16)
-    up_ref[0] = tn(x, act_ref[2]).astype(BF16)
-    down_ref[0] = tn(act_ref[0], s).astype(BF16)
+    swap.wait_recv()
+    grad_ref[...] = (last_mine[...] + last_in[...].astype(F32)).astype(BF16)
+    swap.wait_send()
+
+    def settle_grads(n, carry):
+        for half in range(2):
+            grad_out(n, half).wait()
+        return carry
+
+    lax.fori_loop(3 * PIECES - SLOTS_OUT, 3 * PIECES, settle_grads, 0)
 
 
 def shards(tokens, cotangent, route_scale, expert_index, gate_matrix, up_matrix, down_matrix):
@@ -348,19 +380,18 @@
     chunks = experts // group
     depth = group * capacity
     any_, vmem, dma = pl.ANY, pltpu.VMEM, pltpu.SemaphoreType.DMA
-    token_grad, slot_rows, acts = pl.pallas_call(
+    token_grad, weight_grads = pl.pallas_call(
         functools.partial(exchange_kernel, capacity),
         out_shape=(
             jax.ShapeDtypeStruct((rows_here, width), BF16),
-            jax.ShapeDtypeStruct((2, PIECES, slots, wide), BF16),
-            jax.ShapeDtypeStruct((3, slots, hidden), BF16),
+            jax.ShapeDtypeStruct((3, hidden, features), BF16),
         ),
         in_specs=[pl.BlockSpec(memory_space=vmem)] * 2 + [pl.BlockSpec(memory_space=any_)] * 5,
-        out_specs=(pl.BlockSpec(memory_space=vmem), pl.BlockSpec(memory_space=any_), pl.BlockSpec(memory_space=any_)),
+        out_specs=(pl.BlockSpec(memory_space=vmem), pl.BlockSpec(memory_space=any_)),
         scratch_shapes=[
             vmem((2, PIECES, slots, wide), BF16),
-            vmem((PIECES, wide, hidden), BF16),
-            vmem((PIECES, wide, hidden), BF16),
+            vmem((PIECES, hidden, wide), BF16),
+            vmem((PIECES, hidden, wide), BF16),
             vmem((PIECES, hidden, wide), BF16),
             vmem((2, rows_here, wide), BF16),
             vmem((experts, 2, capacity, wide), BF16),
@@ -376,8 +407,11 @@
             vmem((slots, wide), BF16),
             vmem((slots, wide), BF16),
             vmem((slots, wide), BF16),
+            vmem((rows_here, width), F32),
             vmem((rows_here, width), BF16),
             vmem((rows_here, width), BF16),
+            vmem((3, hidden, slots), BF16),
+            vmem((SLOTS_OUT, hidden, wide), BF16),
             dma((2, 2)),
             dma((3, 2, PIECES)),
             dma((experts,)),
@@ -393,43 +427,19 @@
             dma((experts,)),
             dma((experts,)),
             dma((2,)),
-            dma((3, chunks)),
+            dma((SLOTS_OUT, 2)),
         ],
         compiler_params=pltpu.CompilerParams(
             collective_id=0, has_side_effects=True, vmem_limit_bytes=56 * 2**20
         ),
         cost_estimate=pl.CostEstimate(
-            flops=10 * slots * features * hidden,
-            bytes_accessed=6 * features * hidden + 4 * slots * features,
+            flops=16 * slots * features * hidden,
+            bytes_accessed=12 * features * hidden,
             transcendentals=slots * hidden,
         ),
-    )(expert_index, route_scale, tokens, cotangent, gate_matrix, up_matrix, down_matrix)
-    gate_grad, up_grad, down_grad = pl.pallas_call(
-        weight_grads_kernel,
-        grid=(8,),
-        out_shape=(
-            jax.ShapeDtypeStruct((1, features, hidden), BF16),
-            jax.ShapeDtypeStruct((1, features, hidden), BF16),
-            jax.ShapeDtypeStruct((1, hidden, features), BF16),
-        ),
-        in_specs=[
-            pl.BlockSpec((1, 1, slots, width), lambda i: (0, lax.rem(i, 4), 0, lax.div(i, 4))),
-            pl.BlockSpec((1, 1, slots, width), lambda i: (1, lax.rem(i, 4), 0, lax.div(i, 4))),
-            pl.BlockSpec((3, slots, hidden), lambda i: (0, 0, 0)),
-        ],
-        out_specs=(
-            pl.BlockSpec((1, width, hidden), lambda i: (0, i, 0)),
-            pl.BlockSpec((1, width, hidden), lambda i: (0, i, 0)),
-            pl.BlockSpec((1, hidden, width), lambda i: (0, 0, i)),
-        ),
-        compiler_params=pltpu.CompilerParams(vmem_limit_bytes=48 * 2**20),
-        cost_estimate=pl.CostEstimate(
-            flops=6 * slots * features * hidden,
-            bytes_accessed=6 * features * hidden + 4 * slots * features,
-            transcendentals=0,
-        ),
-    )(slot_rows, slot_rows, acts)
-    return token_grad, gate_grad, up_grad, down_grad
+    )(expert_index.T, route_scale.T, tokens, cotangent, jnp.swapaxes(gate_matrix, 1, 2), jnp.swapaxes(up_matrix, 1, 2), down_matrix)
+    down_grad, gate_grad, up_grad = weight_grads[0:1], weight_grads[1:2], weight_grads[2:3]
+    return token_grad, jnp.swapaxes(gate_grad, 1, 2), jnp.swapaxes(up_grad, 1, 2), down_grad
 
 
 def solution(mesh):

time: 146 us -> 95.8 us (0.66)
  Pallas kernels: 112 us -> 84.3 us
  local copies, waits for them, and re-layouts: 31.2 us -> 9.64 us
    unnamed x11 -> x3, local copies, waits for them, and re-layouts: 31.2 us -> 0.64 us
    pallas_call x1 -> x0, Pallas kernels: 15.4 us -> none  [shards(): pl.pallas_call(weight_grads_kernel, grid=(8,), out_shape=(jax.ShapeDtypeS...]
    pallas_call x1, Pallas kernels: 96.9 us -> 84.3 us  [shards(): pl.pallas_call(functools.partial(exchange_kernel, capacity), out_shape=(j...]
    slice x0 -> x1, local copies, waits for them, and re-layouts: none -> 9 us  [shards(): weight_grads[0:1]]
where the time goes in v2:
time: 95.8 us; the launch traced here: 94.6 us
  Pallas kernels  84.3 us (88%)
  local copies, waits for them, and re-layouts  9.64 us (10%)
    pallas_call x1, Pallas kernels, shards(): pl.pallas_call(functools.partial(exchange_kernel, capacity), out_shape=(j...  84.3 us
    slice x1, local copies, waits for them, and re-layouts, shards(): weight_grads[0:1]  9 us

profile of v2, /device:TPU:0, one launch (start us, length us, event | category | flops | bytes accessed | tf_op | source)
XLA Modules:
  0.0 94.6 jit_solution(7923957740075763376)
XLA Ops:
  0.6 84.3 %shard_map.102 = (bf16[128,384]{1,0:T(8,128)(2,1)}, bf16[3,672,3072]{2,1,0:T(8,128)(2,1)}) custom-call(s32[4,128]{1,0:T(4,128)} %bitcast.10, f32[4,128]{1,0:T(4,128)} %bitcast.11, bf16[128,3072]{1,0:T(8,128)(2,1)} %tok_hbm.1, bf16[128,3072]{1,0:T(8,128)(2,1)} %cot_hbm.1, bf16[1,672,3072]{2,1,0:T(8,128)(2,1)} %bitcast.8, bf16[1,672,3072]{2,1,0:T(8,128)(2,1)} %bitcast.9, ...), custom_call_target="tpu_custom_call" | custom-call | flops 25367150592 | bytes 24772608 | tf_op jit(solution)/shard_map/pallas_call | solution.py:383
  85.0 0.0 copy-start
  85.0 9.0 %fusion = (bf16[1,672,3072]{2,1,0:T(8,128)(2,1)}, bf16[1,3072,672]{1,2,0:T(8,128)(2,1)}, bf16[1,3072,672]{1,2,0:T(8,128)(2,1)}) fusion(bf16[3,672,3072]{2,1,0:T(8,128)(2,1)} %get-tuple-element.7), kind=kLoop, calls=%fused_computation.2 | loop fusion | bytes 24772608 | tf_op jit(solution)/shard_map/slice | solution.py:441
  94.0 0.0 copy-done
  94.0 0.6 copy.12
Async XLA Ops:
  85.0 9.0 %copy-start = (bf16[128,384]{1,0:T(8,128)(2,1)S(1)}, bf16[128,384]{1,0:T(8,128)(2,1)}, u32[]{:S(2)}) copy-start(bf16[128,384]{1,0:T(8,128)(2,1)} %get-tuple-element.15) | copy-start | bytes 294916

commit v3 on v2

--- a/solution.py
+++ b/solution.py
@@ -9,10 +9,14 @@
 
 PIECES = 4
 GRID = 4
-AHEAD = 5
+AHEAD = 6
+MOVES = (
+    (0, 0), (1, 0), (3, 0), (0, 1), (0, 3), (2, 0), (0, 2), (2, 2),
+    (2, 1), (2, 3), (1, 2), (3, 2), (1, 1), (3, 3), (1, 3), (3, 1),
+)
 RELAY_LAG = 3
 SLOTS_OUT = 4
-CUTS = (3, 8)
+CUTS = (0, 4)
 BF16 = jnp.bfloat16
 F32 = jnp.float32
 
@@ -32,8 +36,10 @@
 def shifted(me, step, count, sign):
     if count != GRID * GRID:
         return lax.rem(me + sign * step + count, count)
-    first = lax.rem(step, GRID)
-    second = lax.rem(first + lax.div(step, GRID), GRID)
+    move = 0
+    for k, (dx, dz) in enumerate(MOVES):
+        move = jnp.where(step == k, dx * GRID + dz, move)
+    first, second = lax.div(move, GRID), lax.rem(move, GRID)
     row = lax.rem(lax.div(me, GRID) + sign * first + GRID, GRID)
     column = lax.rem(lax.rem(me, GRID) + sign * second + GRID, GRID)
     return row * GRID + column
@@ -42,11 +48,11 @@
 def exchange_kernel(
     capacity,
     index_ref, scale_ref, tok_hbm, cot_hbm, gate_hbm, up_hbm, down_hbm,
-    grad_ref, weights_hbm,
-    rows, gate_v, up_v, down_v, piece, stage, select, rank, weight, total, act,
-    to_pair, from_pair, to_y, keep, from_y, final, back, last_mine, last_out, last_in, turned, made,
+    grad_ref, other_ref, weights_hbm, tokens_out_hbm, behind_hbm,
+    rows, weights_v, piece, stage, select, rank, weight, total, act,
+    to_pair, from_pair, to_y, keep, from_y, final, back, turned, made,
     piece_sem, load_sem, xz_s, xz_r, pair_s, pair_r, y_s, y_r, rp_s, rp_r, ry_s, ry_r, rx_s, rx_r,
-    last_sem, out_sem,
+    out_sem, pass_sem,
 ):
     count = lax.axis_size("aa")
     tokens = tok_hbm.shape[0]
@@ -57,6 +63,7 @@
     group = count // 4 if count >= 4 else 1
     chunks = count // group
     depth = group * capacity
+    parts = 2 if group % 2 == 0 else 1
     me = lax.axis_index("aa")
     b = lax.axis_index("ba")
     y, c = lax.div(b, 2), lax.rem(b, 2)
@@ -93,8 +100,8 @@
         for half in range(2):
             far = (p + 4 * half) * width
             near = half * width
-            for k, (source, target) in enumerate(((gate_hbm, gate_v), (up_hbm, up_v), (down_hbm, down_v))):
-                made.append(pltpu.make_async_copy(source.at[0, :, pl.ds(far, width)], target.at[p, :, pl.ds(near, width)], load_sem.at[k, half, p]))
+            for k, source in enumerate((gate_hbm, up_hbm, down_hbm)):
+                made.append(pltpu.make_async_copy(source.at[0, :, pl.ds(far, width)], weights_v.at[k, p, :, pl.ds(near, width)], load_sem.at[k, half, p]))
         return made
 
     labels = lax.broadcasted_iota(jnp.int32, (count, tokens), 0)
@@ -133,32 +140,29 @@
     def sum_core(k, q):
         return remote(to_pair.at[k, chunk(q), :], from_pair.at[k, chunk(q), :], rp_s.at[k, q], rp_r.at[k, q], ba=pair)
 
-    def sum_plane(k, q):
+    def portion(i):
+        return pl.ds(pl.multiple_of(i * (depth // parts), 16), depth // parts)
+
+    def sum_plane(k, i):
         half = pl.ds(k * width, width)
-        return remote(to_y.at[chunk(q), half], from_y.at[chunk(q), half], ry_s.at[k, q], ry_r.at[k, q], ba=(before, after)[k])
+        return remote(to_y.at[portion(i), half], from_y.at[portion(i), half], ry_s.at[k, i], ry_r.at[k, i], ba=(before, after)[k])
 
     def home(o):
         return remote(final.at[block(o), :], back.at[block(o), :], rx_s.at[o], rx_r.at[o], aa=shifted(me, o, count, -1))
 
-    def grad_out(n, half):
-        k, p = lax.rem(n, 3), lax.div(n, 3)
+    def tokens_out(q):
+        return pltpu.make_async_copy(rows.at[0, :, chunk(q), :], tokens_out_hbm.at[:, chunk(q), :], pass_sem.at[0, q])
+
+    def behind_out(k):
+        return pltpu.make_async_copy(turned.at[k + 1], behind_hbm.at[k], pass_sem.at[1, k])
+
+    def grad_out(n):
         slot = lax.rem(n, SLOTS_OUT)
-        there = pl.ds(pl.multiple_of((p + 4 * half) * width, 128), width)
-        return pltpu.make_async_copy(
-            made.at[slot, :, pl.ds(half * width, width)], weights_hbm.at[k, :, there], out_sem.at[slot, half])
+        return pltpu.make_async_copy(made.at[slot], weights_hbm.at[n], out_sem.at[slot])
 
     def grad_step(n, carry):
-        k, p = lax.rem(n, 3), lax.div(n, 3)
-
-        @pl.when(n >= SLOTS_OUT)
-        def _():
-            for half in range(2):
-                grad_out(n - SLOTS_OUT, half).wait()
-
-        side = jnp.where(k == 0, 1, 0)
-        made[lax.rem(n, SLOTS_OUT)] = nn(turned[k], rows[side, p]).astype(BF16)
-        for half in range(2):
-            grad_out(n, half).start()
+        made[lax.rem(n, SLOTS_OUT)] = nn(turned[0], rows[1, n]).astype(BF16)
+        grad_out(n).start()
         return carry
 
     def grads(first, last):
@@ -167,11 +171,6 @@
     for array in range(2):
         for half in range(2):
             piece_load(array, half).wait()
-    for p in range(PIECES):
-        for load in weight_loads(p):
-            load.start()
-    pl.semaphore_wait(barrier, count - 1 + 4)
-
     def dispatch(step, carry):
         o = lax.rem(step + 1, count)
         expert = shifted(me, o, count, 1)
@@ -183,33 +182,34 @@
         stage[o, 0] = nn(picks, piece[0]).astype(BF16)
         stage[o, 1] = (scale * nn(picks, piece[1])).astype(BF16)
 
-        @pl.when((o > 0) & (o < AHEAD))
-        def _():
-            xz(o).start()
-
-        @pl.when(o == 0)
-        def _():
-            for a in range(2):
-                rows[a, own, 0:capacity, :] = stage[0, a]
-
-        return carry
-
-    lax.fori_loop(0, count, dispatch, 0)
+        return carry
+
+    def first_sends(o, carry):
+        xz(o).start()
+        return carry
+
+    ahead = min(AHEAD, count)
+    lax.fori_loop(0, ahead - 1, dispatch, 0)
+    pl.semaphore_wait(barrier, count - 1 + 4)
+    lax.fori_loop(1, ahead, first_sends, 0)
+    lax.fori_loop(ahead - 1, count, dispatch, 0)
+    for a in range(2):
+        rows[a, own, 0:capacity, :] = stage[0, a]
     for p in range(PIECES):
         for load in weight_loads(p):
-            load.wait()
+            load.start()
 
     lag_c = group + RELAY_LAG + 1
     lag_d = lag_c + 4
-    lag_e = lag_d + 6
-    steps = lag_d + 4 * chunks
-
-    def send_home(q):
-        sum_plane(0, q).wait_recv()
-        sum_plane(1, q).wait_recv()
-        final[chunk(q), :] = (keep[chunk(q), :] + from_y[chunk(q), :].astype(F32)).astype(BF16)
-        for i in range(group):
-            o = q * group + i
+    lag_e = lag_d + 5
+    steps = lag_d + 4 * chunks - 2
+
+    def send_home(n):
+        sum_plane(0, n).wait_recv()
+        sum_plane(1, n).wait_recv()
+        final[portion(n), :] = (keep[portion(n), :] + from_y[portion(n), :].astype(F32)).astype(BF16)
+        for i in range(group // parts):
+            o = n * (group // parts) + i
 
             @pl.when(o > 0)
             def _():
@@ -218,6 +218,32 @@
             @pl.when(o == 0)
             def _():
                 back[0:capacity, :] = final[0:capacity, :]
+
+    def backward_unit(w, carry):
+        q, j = lax.div(w, 4), lax.rem(w, 4)
+        plane = jnp.where(lax.rem(j, 2) == 0, 1 - h, h)
+        core = jnp.where(j < 2, 1 - c, c)
+        p = 2 * plane + core
+        part = nn(act[1, chunk(q), :], weights_v[0, p]) + nn(act[2, chunk(q), :], weights_v[1, p])
+
+        @pl.when(j < 2)
+        def _():
+            to_pair[j, chunk(q), :] = part.astype(BF16)
+            sum_core(j, q).start()
+
+        @pl.when(j == 2)
+        def _():
+            sum_core(0, q).wait_recv()
+            to_y[chunk(q), :] = (part + from_pair[0, chunk(q), :].astype(F32)).astype(BF16)
+            for i in range(parts):
+                sum_plane(0, q * parts + i).start()
+                sum_plane(1, q * parts + i).start()
+
+        @pl.when(j == 3)
+        def _():
+            sum_core(1, q).wait_recv()
+            keep[chunk(q), :] = part + from_pair[1, chunk(q), :].astype(F32)
+        return carry
 
     def main(t, carry):
         @pl.when(t < count)
@@ -252,17 +278,23 @@
         def _():
             q, j = lax.div(v, 4), lax.rem(v, 4)
 
+            @pl.when(v == 0)
+            def _():
+                for p in range(PIECES):
+                    for load in weight_loads(p):
+                        load.wait()
+
             @pl.when(j == 0)
             def _():
                 for i in range(group):
                     to_core(0, q * group + i).wait_recv()
                     to_core(1, q * group + i).wait_recv()
-                total[...] = jnp.zeros_like(total)
-
-            x = rows[0, j, chunk(q), :]
-            total[0] += nt(x, gate_v[j])
-            total[1] += nt(x, up_v[j])
-            total[2] += nt(rows[1, j, chunk(q), :], down_v[j])
+                tokens_out(q).start()
+
+            @pl.when(j < 3)
+            def _():
+                side = jnp.where(j == 2, 1, 0)
+                total[j] = sum(nt(rows[side, p, chunk(q), :], weights_v[j, p]) for p in range(PIECES))
 
             @pl.when(j == 3)
             def _():
@@ -275,62 +307,45 @@
 
         w = t - lag_d
 
-        @pl.when((w >= 0) & (w < 4 * chunks))
-        def _():
-            q, j = lax.div(w, 4), lax.rem(w, 4)
-            plane = jnp.where(lax.rem(j, 2) == 0, 1 - h, h)
-            core = jnp.where(j < 2, 1 - c, c)
-            p = 2 * plane + core
-            part = nn(act[1, chunk(q), :], gate_v[p]) + nn(act[2, chunk(q), :], up_v[p])
-
-            @pl.when(j < 2)
-            def _():
-                to_pair[j, chunk(q), :] = part.astype(BF16)
-                sum_core(j, q).start()
-
-            @pl.when(j == 2)
-            def _():
-                sum_core(0, q).wait_recv()
-                to_y[chunk(q), :] = (part + from_pair[0, chunk(q), :].astype(F32)).astype(BF16)
-                sum_plane(0, q).start()
-                sum_plane(1, q).start()
-
-            @pl.when(j == 3)
-            def _():
-                sum_core(1, q).wait_recv()
-                keep[chunk(q), :] = part + from_pair[1, chunk(q), :].astype(F32)
+        @pl.when((w >= 0) & (w < 4 * chunks - 2))
+        def _():
+            backward_unit(w, 0)
 
         z = t - lag_e
 
         @pl.when((z >= 0) & (z < 4 * (chunks - 1)) & (lax.rem(z + 4, 4) == 0))
         def _():
-            send_home(lax.div(z, 4))
+            for i in range(parts):
+                send_home(lax.div(z, 4) * parts + i)
 
         return carry
 
     lax.fori_loop(0, steps, main, 0)
 
-    def turn(k, carry):
-        turned[k] = act[k].T
-        return carry
-
-    lax.fori_loop(0, 3, turn, 0)
+    turned[0] = act[0].T
+    lax.fori_loop(4 * chunks - 2, 4 * chunks, backward_unit, 0)
+    for k in range(2):
+        turned[k + 1] = act[k + 1].T
+        behind_out(k).start()
     grads(0, CUTS[0])
-    send_home(chunks - 1)
-    grads(CUTS[0], CUTS[1])
+    for i in range(parts):
+        send_home(jnp.int32((chunks - 1) * parts + i))
+        grads(CUTS[0] + i, CUTS[0] + i + 1)
+    grads(CUTS[0] + parts, CUTS[1])
 
     def arrive(o, carry):
         home(o).wait_recv()
         return carry
 
-    lax.fori_loop(1, count, arrive, 0)
-    merged = tn(select[...], back[...])
+    early = (chunks - 1) * depth
+    lax.fori_loop(1, count - group, arrive, 0)
+    keep[0:tokens, :] = tn(select[0:early, :], back[0:early, :])
+    lax.fori_loop(count - group, count, arrive, 0)
+    merged = keep[0:tokens, :] + tn(select[early:slots, :], back[early:slots, :])
     low, high = merged[:, :width], merged[:, width:]
-    last_out[...] = jnp.where(y < 2, high, low).astype(BF16)
-    last_mine[...] = jnp.where(y < 2, low, high)
-    swap = remote(last_out, last_in, last_sem.at[0], last_sem.at[1], ba=across)
-    swap.start()
-    grads(CUTS[1], 3 * PIECES)
+    grad_ref[...] = jnp.where(y < 2, low, high)
+    other_ref[...] = jnp.where(y < 2, high, low).astype(BF16)
+    grads(CUTS[1], PIECES)
 
     def settle(o, carry):
         @pl.when((o > 0) & (o >= count - AHEAD))
@@ -349,22 +364,59 @@
     lax.fori_loop(0, count, settle, 0)
 
     def settle_sums(q, carry):
+        tokens_out(q).wait()
         for k in range(2):
             sum_core(k, q).wait_send()
-            sum_plane(k, q).wait_send()
+            for i in range(parts):
+                sum_plane(k, q * parts + i).wait_send()
         return carry
 
     lax.fori_loop(0, chunks, settle_sums, 0)
-    swap.wait_recv()
-    grad_ref[...] = (last_mine[...] + last_in[...].astype(F32)).astype(BF16)
-    swap.wait_send()
+    for k in range(2):
+        behind_out(k).wait()
 
     def settle_grads(n, carry):
+        grad_out(n).wait()
+        return carry
+
+    lax.fori_loop(PIECES - SLOTS_OUT, PIECES, settle_grads, 0)
+
+
+def finish_kernel(rows_hbm, behind_hbm, held_hbm, gate_hbm, up_hbm, down_hbm, turned, rows, made, load_sems, sems):
+    width = rows.shape[2] // 2
+
+    def load(k, step):
+        source, target = ((rows_hbm, rows), (held_hbm, made.at[2]))[k]
+        return pltpu.make_async_copy(source.at[step], target.at[step], load_sems.at[k, step])
+
+    def outs(k, step):
         for half in range(2):
-            grad_out(n, half).wait()
-        return carry
-
-    lax.fori_loop(3 * PIECES - SLOTS_OUT, 3 * PIECES, settle_grads, 0)
+            target = (gate_hbm, up_hbm, down_hbm)[k]
+            yield pltpu.make_async_copy(
+                made.at[k, step, :, pl.ds(half * width, width)],
+                target.at[0, :, pl.ds((step + 4 * half) * width, width)],
+                sems.at[k, step, half],
+            )
+
+    first = pltpu.make_async_copy(behind_hbm, turned, load_sems.at[2, 0])
+    first.start()
+    for step in range(PIECES):
+        for k in range(2):
+            load(k, step).start()
+    first.wait()
+    for step in range(PIECES):
+        load(1, step).wait()
+        for copy in outs(2, step):
+            copy.start()
+        load(0, step).wait()
+        for k in range(2):
+            made[k, step] = nn(turned[k], rows[step]).astype(BF16)
+            for copy in outs(k, step):
+                copy.start()
+    for k in range(3):
+        for step in range(PIECES):
+            for copy in outs(k, step):
+                copy.wait()
 
 
 def shards(tokens, cotangent, route_scale, expert_index, gate_matrix, up_matrix, down_matrix):
@@ -380,19 +432,20 @@
     chunks = experts // group
     depth = group * capacity
     any_, vmem, dma = pl.ANY, pltpu.VMEM, pltpu.SemaphoreType.DMA
-    token_grad, weight_grads = pl.pallas_call(
+    mine, other, held, slot_rows, behind = pl.pallas_call(
         functools.partial(exchange_kernel, capacity),
         out_shape=(
+            jax.ShapeDtypeStruct((rows_here, width), F32),
             jax.ShapeDtypeStruct((rows_here, width), BF16),
-            jax.ShapeDtypeStruct((3, hidden, features), BF16),
+            jax.ShapeDtypeStruct((PIECES, hidden, wide), BF16),
+            jax.ShapeDtypeStruct((PIECES, slots, wide), BF16),
+            jax.ShapeDtypeStruct((2, hidden, slots), BF16),
         ),
         in_specs=[pl.BlockSpec(memory_space=vmem)] * 2 + [pl.BlockSpec(memory_space=any_)] * 5,
-        out_specs=(pl.BlockSpec(memory_space=vmem), pl.BlockSpec(memory_space=any_)),
+        out_specs=(pl.BlockSpec(memory_space=vmem), pl.BlockSpec(memory_space=vmem)) + (pl.BlockSpec(memory_space=any_),) * 3,
         scratch_shapes=[
             vmem((2, PIECES, slots, wide), BF16),
-            vmem((PIECES, hidden, wide), BF16),
-            vmem((PIECES, hidden, wide), BF16),
-            vmem((PIECES, hidden, wide), BF16),
+            vmem((3, PIECES, hidden, wide), BF16),
             vmem((2, rows_here, wide), BF16),
             vmem((experts, 2, capacity, wide), BF16),
             vmem((slots, rows_here), BF16),
@@ -407,9 +460,6 @@
             vmem((slots, wide), BF16),
             vmem((slots, wide), BF16),
             vmem((slots, wide), BF16),
-            vmem((rows_here, width), F32),
-            vmem((rows_here, width), BF16),
-            vmem((rows_here, width), BF16),
             vmem((3, hidden, slots), BF16),
             vmem((SLOTS_OUT, hidden, wide), BF16),
             dma((2, 2)),
@@ -422,23 +472,43 @@
             dma((2, experts)),
             dma((2, chunks)),
             dma((2, chunks)),
-            dma((2, chunks)),
-            dma((2, chunks)),
+            dma((2, 2 * chunks)),
+            dma((2, 2 * chunks)),
             dma((experts,)),
             dma((experts,)),
-            dma((2,)),
-            dma((SLOTS_OUT, 2)),
+            dma((SLOTS_OUT,)),
+            dma((2, chunks)),
         ],
         compiler_params=pltpu.CompilerParams(
             collective_id=0, has_side_effects=True, vmem_limit_bytes=56 * 2**20
         ),
         cost_estimate=pl.CostEstimate(
-            flops=16 * slots * features * hidden,
+            flops=12 * slots * features * hidden,
             bytes_accessed=12 * features * hidden,
             transcendentals=slots * hidden,
         ),
     )(expert_index.T, route_scale.T, tokens, cotangent, jnp.swapaxes(gate_matrix, 1, 2), jnp.swapaxes(up_matrix, 1, 2), down_matrix)
-    down_grad, gate_grad, up_grad = weight_grads[0:1], weight_grads[1:2], weight_grads[2:3]
+    swapped = lax.ppermute(other, "ba", [(i, (i + 4) % 8) for i in range(8)])
+    token_grad = (mine + swapped.astype(F32)).astype(BF16)
+    gate_grad, up_grad, down_grad = pl.pallas_call(
+        finish_kernel,
+        out_shape=[jax.ShapeDtypeStruct((1, hidden, features), BF16)] * 3,
+        in_specs=[pl.BlockSpec(memory_space=any_)] * 3,
+        out_specs=[pl.BlockSpec(memory_space=any_)] * 3,
+        scratch_shapes=[
+            vmem((2, hidden, slots), BF16),
+            vmem((PIECES, slots, wide), BF16),
+            vmem((3, PIECES, hidden, wide), BF16),
+            dma((3, PIECES)),
+            dma((3, PIECES, 2)),
+        ],
+        compiler_params=pltpu.CompilerParams(vmem_limit_bytes=56 * 2**20),
+        cost_estimate=pl.CostEstimate(
+            flops=4 * slots * features * hidden,
+            bytes_accessed=8 * features * hidden + 2 * slots * features,
+            transcendentals=0,
+        ),
+    )(slot_rows, behind, held)
     return token_grad, jnp.swapaxes(gate_grad, 1, 2), jnp.swapaxes(up_grad, 1, 2), down_grad
 
 

time: 95.8 us -> 93.6 us (0.977)
  local copies, waits for them, and re-layouts: 9.64 us -> 0.01 us
  Pallas kernels: 84.3 us -> 90.3 us
  starting transfers between devices: 0 us -> 1.72 us
    pallas_call x0 -> x1, Pallas kernels: none -> 10.7 us  [shards(): pl.pallas_call(finish_kernel, out_shape=[jax.ShapeDtypeStruct((1, hidden,...]
    slice x1 -> x0, local copies, waits for them, and re-layouts: 9 us -> none  [shards(): weight_grads[0:1]]
    pallas_call x1, Pallas kernels: 84.3 us -> 79.6 us  [shards(): pl.pallas_call(functools.partial(exchange_kernel, capacity), out_shape=(j...]
    ppermute x0 -> x1, starting transfers between devices: none -> 1.72 us  [shards(): swapped = lax.ppermute(other, 'ba', [(i, (i + 4) % 8) for i in range(8)])]
  transfers between devices with their start and end apart: 0 -> 1, of which waited for: 0 -> 0; matrix products, arithmetic and copies ran while one was open for 0% -> 0% of each run, Pallas kernels for 0% -> 11%
where the time goes in v3:
time: 93.6 us; the launch traced here: 93.4 us
  Pallas kernels  90.3 us (96%)
  starting transfers between devices  1.72 us (2%)
    pallas_call x1, Pallas kernels, shards(): pl.pallas_call(functools.partial(exchange_kernel, capacity), out_shape=(j...  79.6 us
    pallas_call x1, Pallas kernels, shards(): pl.pallas_call(finish_kernel, out_shape=[jax.ShapeDtypeStruct((1, hidden,...  10.7 us
  transfers between devices with their start and end apart: 1, of which 0 were waited for; matrix products, arithmetic and copies ran while one was open for 0% of the time, Pallas kernels for 11%

profile of v3, /device:TPU:0, one launch (start us, length us, event | category | flops | bytes accessed | tf_op | source)
XLA Modules:
  0.0 93.4 jit_solution(10097278466346748697)
XLA Ops:
  0.6 79.6 %shard_map.102 = (f32[128,384]{1,0:T(8,128)}, bf16[128,384]{1,0:T(8,128)(2,1)}, bf16[4,672,768]{2,1,0:T(8,128)(2,1)}, bf16[4,768,768]{2,1,0:T(8,128)(2,1)}, bf16[2,672,768]{2,1,0:T(8,128)(2,1)}) custom-call(s32[4,128]{1,0:T(4,128)} %bitcast.8, f32[4,128]{1,0:T(4,128)} %bitcast.9, bf16[128,3072]{1,0:T(8,128)(2,1)} %tok_hbm.1, bf16[128,3072]{1,0:T(8,128)(2,1)} %cot_hbm.1, ...), custom_call_target="tpu_custom_call" | custom-call | flops 19025362944 | bytes 24772608 | tf_op jit(solution)/shard_map/pallas_call | solution.py:435
  80.3 1.7 %collective-permute-start = (bf16[128,384]{1,0:T(8,128)(2,1)}, bf16[128,384]{1,0:T(8,128)(2,1)S(1)}, u32[]{:S(2)}, u32[]{:S(2)}) collective-permute-start(bf16[128,384]{1,0:T(8,128)(2,1)} %get-tuple-element.13), channel_id=1, source_target_pairs={{0,4},{1,5},{2,6},{3,7},{4,0},{5,1},{6,2},{7,3},{8,12},{9,13},{10,... | collective-permute-start | bytes 294920 | tf_op jit(solution)/shard_map/ppermute | solution.py:491
  82.0 0.0 copy-start
  82.0 10.7 %shard_map.103 = (bf16[1,672,3072]{2,1,0:T(8,128)(2,1)}, bf16[1,672,3072]{2,1,0:T(8,128)(2,1)}, bf16[1,672,3072]{2,1,0:T(8,128)(2,1)}) custom-call(bf16[4,768,768]{2,1,0:T(8,128)(2,1)} %get-tuple-element.14.rows_hbm, bf16[2,672,768]{2,1,0:T(8,128)(2,1)} %get-tuple-element.15.behind_hbm, bf16[4,672,768]{2,1,0:T(8,128)(2,1)} %get-tuple-element.16.held_hbm), custom_call_target="tpu_custom_call" | custom-call | flops 6341787648 | bytes 21233664 | tf_op jit(solution)/shard_map/pallas_call | solution.py:493
  92.7 0.0 collective-permute-done
  92.7 0.0 copy-done
  92.7 0.7 add_convert_fusion
Async XLA Ops:
  80.3 12.5 %collective-permute-start = (bf16[128,384]{1,0:T(8,128)(2,1)}, bf16[128,384]{1,0:T(8,128)(2,1)S(1)}, u32[]{:S(2)}, u32[]{:S(2)}) collective-permute-start(bf16[128,384]{1,0:T(8,128)(2,1)} %get-tuple-element.13), channel_id=1, source_target_pairs={{0,4},{1,5},{2,6},{3,7},{4,0},{5,1},{6,2},{7,3},{8,12},{9,13},{10,... | collective-permute-start | bytes 294920 | tf_op jit(solution)/shard_map/ppermute | solution.py:491
  82.0 10.7 %copy-start = (f32[128,384]{1,0:T(8,128)S(1)}, f32[128,384]{1,0:T(8,128)}, u32[]{:S(2)}) copy-start(f32[128,384]{1,0:T(8,128)} %get-tuple-element.12) | copy-start | bytes 589828

commit v4 on v3

--- a/solution.py
+++ b/solution.py
@@ -200,7 +200,7 @@
             load.start()
 
     lag_c = group + RELAY_LAG + 1
-    lag_d = lag_c + 4
+    lag_d = lag_c + 3
     lag_e = lag_d + 5
     steps = lag_d + 4 * chunks - 2
 
@@ -296,7 +296,7 @@
                 side = jnp.where(j == 2, 1, 0)
                 total[j] = sum(nt(rows[side, p, chunk(q), :], weights_v[j, p]) for p in range(PIECES))
 
-            @pl.when(j == 3)
+            @pl.when(j == 2)
             def _():
                 gate, up, behind = total[0], total[1], total[2]
                 sigmoid = jax.nn.sigmoid(gate)

time: 93.6 us -> 92.9 us (level)
  transfers between devices with their start and end apart: 1 -> 1, of which waited for: 0 -> 0; matrix products, arithmetic and copies ran while one was open for 0% -> 0% of each run, Pallas kernels for 11% -> 12%
where the time goes in v4:
time: 92.9 us; the launch traced here: 92.8 us
  Pallas kernels  89.7 us (97%)
  starting transfers between devices  1.72 us (2%)
    pallas_call x1, Pallas kernels, shards(): pl.pallas_call(functools.partial(exchange_kernel, capacity), out_shape=(j...  79 us
    pallas_call x1, Pallas kernels, shards(): pl.pallas_call(finish_kernel, out_shape=[jax.ShapeDtypeStruct((1, hidden,...  10.7 us
  transfers between devices with their start and end apart: 1, of which 0 were waited for; matrix products, arithmetic and copies ran while one was open for 0% of the time, Pallas kernels for 12%

profile of v4, /device:TPU:0, one launch (start us, length us, event | category | flops | bytes accessed | tf_op | source)
XLA Modules:
  0.0 92.8 jit_solution(5986081957652964656)
XLA Ops:
  0.6 79.0 %shard_map.102 = (f32[128,384]{1,0:T(8,128)}, bf16[128,384]{1,0:T(8,128)(2,1)}, bf16[4,672,768]{2,1,0:T(8,128)(2,1)}, bf16[4,768,768]{2,1,0:T(8,128)(2,1)}, bf16[2,672,768]{2,1,0:T(8,128)(2,1)}) custom-call(s32[4,128]{1,0:T(4,128)} %bitcast.8, f32[4,128]{1,0:T(4,128)} %bitcast.9, bf16[128,3072]{1,0:T(8,128)(2,1)} %tok_hbm.1, bf16[128,3072]{1,0:T(8,128)(2,1)} %cot_hbm.1, ...), custom_call_target="tpu_custom_call" | custom-call | flops 19025362944 | bytes 24772608 | tf_op jit(solution)/shard_map/pallas_call | solution.py:435
  79.6 1.7 %collective-permute-start = (bf16[128,384]{1,0:T(8,128)(2,1)}, bf16[128,384]{1,0:T(8,128)(2,1)S(1)}, u32[]{:S(2)}, u32[]{:S(2)}) collective-permute-start(bf16[128,384]{1,0:T(8,128)(2,1)} %get-tuple-element.13), channel_id=1, source_target_pairs={{0,4},{1,5},{2,6},{3,7},{4,0},{5,1},{6,2},{7,3},{8,12},{9,13},{10,... | collective-permute-start | bytes 294920 | tf_op jit(solution)/shard_map/ppermute | solution.py:491
  81.4 0.0 copy-start
  81.4 10.7 %shard_map.103 = (bf16[1,672,3072]{2,1,0:T(8,128)(2,1)}, bf16[1,672,3072]{2,1,0:T(8,128)(2,1)}, bf16[1,672,3072]{2,1,0:T(8,128)(2,1)}) custom-call(bf16[4,768,768]{2,1,0:T(8,128)(2,1)} %get-tuple-element.14.rows_hbm, bf16[2,672,768]{2,1,0:T(8,128)(2,1)} %get-tuple-element.15.behind_hbm, bf16[4,672,768]{2,1,0:T(8,128)(2,1)} %get-tuple-element.16.held_hbm), custom_call_target="tpu_custom_call" | custom-call | flops 6341787648 | bytes 21233664 | tf_op jit(solution)/shard_map/pallas_call | solution.py:493
  92.1 0.0 collective-permute-done
  92.1 0.0 copy-done
  92.1 0.7 add_convert_fusion
Async XLA Ops:
  79.6 12.5 %collective-permute-start = (bf16[128,384]{1,0:T(8,128)(2,1)}, bf16[128,384]{1,0:T(8,128)(2,1)S(1)}, u32[]{:S(2)}, u32[]{:S(2)}) collective-permute-start(bf16[128,384]{1,0:T(8,128)(2,1)} %get-tuple-element.13), channel_id=1, source_target_pairs={{0,4},{1,5},{2,6},{3,7},{4,0},{5,1},{6,2},{7,3},{8,12},{9,13},{10,... | collective-permute-start | bytes 294920 | tf_op jit(solution)/shard_map/ppermute | solution.py:491
  81.4 10.7 %copy-start = (f32[128,384]{1,0:T(8,128)S(1)}, f32[128,384]{1,0:T(8,128)}, u32[]{:S(2)}) copy-start(f32[128,384]{1,0:T(8,128)} %get-tuple-element.12) | copy-start | bytes 589828
